TPU v7x, 32 devices: a whole 2x2x4 slice. The times are simulated.
32 devices in a mesh: grp: 2 (over y), tm: 16 (over z, x, core).
Axes of the slice: x: 2, y: 2, z: 4, core: 2. Of those that a mesh axis runs over, the one named last changes fastest.
Arguments:
- state: float32 [256, 16, 8192], P(('grp', 'tm')), parts along dimension 0, may hold values from -6 to 6
- forcing: float32 [256, 16, 8192], P(('grp', 'tm')), parts along dimension 0, may hold values from -6 to 6
- noise_weight: float32 [256, 8192], P(('grp', 'tm')), parts along dimension 0, may hold values from 0.5 to 2
- prev_coupling: float32 [8192], replicated, may hold values from 0.3 to 1
- next_coupling: float32 [8192], replicated, may hold values from 0.3 to 1
- block_values: bfloat16 [64, 4, 128, 128], replicated, may hold values from -0.25 to 0.25
- block_pattern: int32 [64, 4], replicated, may hold values from 0 to 63, all different within a row
Outputs:
- gradient: float32 [256, 16, 8192], P(('grp', 'tm')), parts along dimension 0
- log_density: float32 [32], P('grp'), parts along dimension 0
There are 2 independent parts, one for each index of `grp`. A program takes and returns all parts, laid end to end along the dimension named above; an argument that names none is the same for every part. Nothing has to cross between parts.
Inputs may be any that keep to these rules, and one draw needn't show every extreme that they name: `block_pattern`: the 4 entries of a row are distinct, and every block is named by some row.
All inputs are finite; a program needn't handle non-finite values.
Results may differ from a plain program's by a relative error of at most 0.0026.
Values sent between devices are 32-bit elements; how exact they have to be, the bound alone decides.
A program may use at most 128 MiB of HBM per device.

v0:
```python
import jax
import jax.numpy as jnp
from jax import lax
from jax.experimental import pallas as pl
from jax.experimental.pallas import tpu as pltpu
from jax.sharding import PartitionSpec as P

MESH = pl.DeviceIdType.MESH
F32 = jnp.float32
BF16 = jnp.bfloat16
LOADS = 8
PIECES = 4


def kernel(
    pat_s, pat_v, pc, nc, state, forcing, weight, values,
    out, dens_out,
    s_v, f_v, w_v, b_v, xr, dr, dual, part, r_first, r_last, w_first, w_last,
    hs_prev, hs_next, hr_prev, hr_next, hw_prev, hw_next, dens, idx_v, idx_s,
    load_sem, b_sem, idx_sem, halo_send, halo_recv, r_send, r_recv, d_send, d_recv,
):
    days, samples, nodes = s_v.shape
    blocks, links, width, _ = b_v.shape
    rows = days * samples
    last = days - 1
    n = lax.axis_size("tm")
    me = lax.axis_index("tm")
    right, left = lax.rem(me + 1, n), lax.rem(me + n - 1, n)

    def cols(i):
        return pl.ds(pl.multiple_of(i * width, width), width)

    loads = [
        pltpu.make_async_copy(state, s_v, load_sem.at[0]),
        pltpu.make_async_copy(forcing, f_v, load_sem.at[1]),
        pltpu.make_async_copy(weight, w_v, load_sem.at[2]),
    ]
    loads[0].start()
    loads[2].start()
    per_load = blocks // LOADS

    def b_load(c):
        span = pl.ds(c * per_load, per_load)
        return pltpu.make_async_copy(values.at[span], b_v.at[span], b_sem.at[c])

    b_load(0).start()
    loads[1].start()
    for c in range(1, LOADS):
        b_load(c).start()

    barrier = pltpu.get_barrier_semaphore()

    @pl.loop(1, n)
    def _(s):
        pl.semaphore_signal(
            barrier, inc=1, device_id={"tm": lax.rem(me + s, n)}, device_id_type=MESH
        )

    pl.semaphore_wait(barrier, n - 1)

    def remote(src, dst, send, recv, target):
        return pltpu.make_async_remote_copy(
            src_ref=src, dst_ref=dst, send_sem=send, recv_sem=recv,
            device_id={"tm": target}, device_id_type=MESH,
        )

    halos = [
        remote(state.at[last], hs_prev, halo_send.at[0], halo_recv.at[0], right),
        remote(state.at[0], hs_next, halo_send.at[1], halo_recv.at[1], left),
    ]
    for copy in halos:
        copy.start()

    lane = lax.broadcasted_iota(jnp.int32, (blocks, blocks), 1)
    sub = lax.broadcasted_iota(jnp.int32, (blocks, blocks), 0)
    none = blocks * links
    idx_v[...] = jnp.zeros_like(idx_v)
    finals = jnp.full((1, blocks), -1, jnp.int32)
    columns = [pat_v[:, k : k + 1] for k in range(links)]
    for k in range(links):
        row = jnp.sum(jnp.where(lane == sub, columns[k], 0), axis=0, keepdims=True)
        found = jnp.full((1, blocks), -1, jnp.int32)
        for q in range(links):
            hit = (columns[q] == row) & (sub < lane)
            found = jnp.maximum(
                found, jnp.max(jnp.where(hit, sub * links + q, -1), axis=0, keepdims=True)
            )
        idx_v[k : k + 1, :blocks] = jnp.where(found < 0, none, found)
        finals = jnp.maximum(
            finals,
            jnp.max(jnp.where(columns[k] == lane, sub * links + k, -1), axis=0, keepdims=True),
        )
    idx_v[links : links + 1, :blocks] = jnp.maximum(finals, 0)
    to_scalar = pltpu.make_async_copy(idx_v, idx_s, idx_sem)
    to_scalar.start()
    part[none] = jnp.zeros((rows, width), F32)

    loads[2].wait()
    w_first[...] = w_v[0:1, :]
    w_last[...] = w_v[last : last + 1, :]
    w_halos = [
        remote(w_last, hw_prev, halo_send.at[2], halo_recv.at[2], right),
        remote(w_first, hw_next, halo_send.at[3], halo_recv.at[3], left),
    ]
    for copy in w_halos:
        copy.start()
    loads[0].wait()

    def round_block(j, _):
        xr[j] = s_v[:, :, cols(j)].reshape(rows, width).astype(BF16)
        return 0

    lax.fori_loop(0, blocks, round_block, 0, unroll=4)
    loads[1].wait()

    def forward(i, total):
        x = jnp.concatenate([xr[pat_s[i, k]] for k in range(links)], axis=1)
        acc = jnp.dot(x, b_v[i].reshape(links * width, width), preferred_element_type=F32)
        acc = acc.reshape(days, samples, width)
        c = cols(i)
        p, q = pc[0:1, c], nc[0:1, c]
        r_first[:, c] = acc[0] - q * s_v[1, :, c] - f_v[0, :, c]
        r_last[:, c] = acc[last] - p * s_v[last - 1, :, c] - f_v[last, :, c]
        for d in range(1, last):
            res = acc[d] - p * s_v[d - 1, :, c] - q * s_v[d + 1, :, c] - f_v[d, :, c]
            du = w_v[d : d + 1, c] * res
            dual[d, :, c] = du
            dr[i, d * samples : (d + 1) * samples, :] = du.astype(BF16)
            total = total + res * du
        return total

    def r_copies(c):
        span = pl.ds(c * (nodes // PIECES), nodes // PIECES)
        return [
            remote(r_last.at[:, span], hr_prev.at[:, span], r_send.at[0, c], r_recv.at[0, c], right),
            remote(r_first.at[:, span], hr_next.at[:, span], r_send.at[1, c], r_recv.at[1, c], left),
        ]

    total = jnp.zeros((samples, width), F32)
    for c in range(LOADS):
        b_load(c).wait()
        total = lax.fori_loop(c * per_load, (c + 1) * per_load, forward, total, unroll=2)
        each = LOADS // PIECES
        if c % each == each - 1:
            for copy in r_copies(c // each):
                copy.start()

    for copy in halos:
        copy.wait_recv()

    def edges(i, total):
        c = cols(i)
        r0 = r_first[:, c] - pc[0:1, c] * hs_prev[:, c]
        r1 = r_last[:, c] - nc[0:1, c] * hs_next[:, c]
        d0 = w_v[0:1, c] * r0
        d1 = w_v[last : last + 1, c] * r1
        dual[0, :, c] = d0
        dual[last, :, c] = d1
        dr[i, 0:samples, :] = d0.astype(BF16)
        dr[i, last * samples :, :] = d1.astype(BF16)
        return total + r0 * d0 + r1 * d1

    total = lax.fori_loop(0, blocks, edges, total, unroll=4)

    sums = -0.5 * jnp.sum(total, axis=1, keepdims=True)
    pick = lax.broadcasted_iota(jnp.int32, (samples, width), 0) == lax.broadcasted_iota(
        jnp.int32, (samples, width), 1
    )
    spread = jnp.sum(jnp.where(pick, sums, 0.0), axis=0, keepdims=True)
    dens[0] = jnp.broadcast_to(spread, dens.shape[1:])

    def d_copy(s):
        return remote(
            dens.at[0], dens.at[s], d_send.at[s], d_recv.at[s], lax.rem(me + s, n)
        )

    @pl.loop(1, n)
    def _(s):
        d_copy(s).start()

    to_scalar.wait()

    def backward(i, _):
        y = lax.dot_general(
            dr[i], b_v[i].reshape(links * width, width),
            (((1,), (1,)), ((), ())), preferred_element_type=F32,
        )
        for k in range(links):
            part[i * links + k] = part[idx_s[k, i]] + y[:, k * width : (k + 1) * width]
        return 0

    lax.fori_loop(0, blocks, backward, 0, unroll=2)

    def gradient(j, _):
        adj = part[idx_s[links, j]].reshape(days, samples, width)
        c = cols(j)
        p, q = pc[0:1, c], nc[0:1, c]
        out[0, :, c] = p * dual[1, :, c] - adj[0]
        out[last, :, c] = q * dual[last - 1, :, c] - adj[last]
        for d in range(1, last):
            out[d, :, c] = p * dual[d + 1, :, c] + q * dual[d - 1, :, c] - adj[d]
        return 0

    lax.fori_loop(0, blocks, gradient, 0, unroll=2)

    for copy in w_halos:
        copy.wait_recv()

    def finish(j, _):
        c = cols(j)
        p, q = pc[0:1, c], nc[0:1, c]
        before = hw_prev[0:1, c] * (hr_prev[:, c] - q * s_v[0, :, c])
        after = hw_next[0:1, c] * (hr_next[:, c] - p * s_v[last, :, c])
        out[0, :, c] = out[0, :, c] + q * before
        out[last, :, c] = out[last, :, c] + p * after
        return 0

    per_piece = blocks // PIECES
    for c in range(PIECES):
        for copy in r_copies(c):
            copy.wait_recv()
        lax.fori_loop(c * per_piece, (c + 1) * per_piece, finish, 0, unroll=4)

    @pl.loop(1, n)
    def _(s):
        d_copy(s).wait()

    def add(s, total):
        return total + dens[s]

    dens_out[...] = lax.fori_loop(1, n, add, dens[0])
    for copy in halos + w_halos:
        copy.wait_send()
    for c in range(PIECES):
        for copy in r_copies(c):
            copy.wait_send()


def shards(state, forcing, noise_weight, prev_coupling, next_coupling, block_values, block_pattern):
    days, samples, nodes = state.shape
    blocks, links, width, _ = block_values.shape
    n = lax.axis_size("tm")
    rows = days * samples
    vmem, sem = pltpu.VMEM, pltpu.SemaphoreType.DMA
    edge = vmem((samples, nodes), F32)
    line = vmem((1, nodes), F32)
    whole = pl.BlockSpec(memory_space=pltpu.VMEM)
    away = pl.BlockSpec(memory_space=pl.ANY)
    gradient, density = pl.pallas_call(
        kernel,
        out_shape=(
            jax.ShapeDtypeStruct((days, samples, nodes), F32),
            jax.ShapeDtypeStruct((8, width), F32),
        ),
        in_specs=[pl.BlockSpec(memory_space=pltpu.SMEM), whole, whole, whole] + [away] * 4,
        out_specs=(whole, whole),
        scratch_shapes=[
            vmem((days, samples, nodes), F32),
            vmem((days, samples, nodes), F32),
            vmem((days, nodes), F32),
            vmem((blocks, links, width, width), BF16),
            vmem((blocks, rows, width), BF16),
            vmem((blocks, rows, width), BF16),
            vmem((days, samples, nodes), F32),
            vmem((blocks * links + 1, rows, width), F32),
            edge, edge, line, line,
            edge, edge, edge, edge, line, line,
            vmem((n, 8, width), F32),
            vmem((8, 128), jnp.int32),
            pltpu.SMEM((8, 128), jnp.int32),
            sem((3,)), sem((LOADS,)), sem,
            sem((4,)), sem((4,)),
            sem((2, PIECES)), sem((2, PIECES)),
            sem((n,)), sem((n,)),
        ],
        compiler_params=pltpu.CompilerParams(
            collective_id=0, has_side_effects=True, vmem_limit_bytes=58 * 2**20
        ),
    )(
        block_pattern, block_pattern,
        prev_coupling.reshape(1, nodes), next_coupling.reshape(1, nodes),
        state, forcing, noise_weight, block_values,
    )
    return gradient, density[0, :samples]


def solution(mesh):
    return jax.shard_map(
        shards,
        mesh=mesh,
        in_specs=(
            P(("grp", "tm"), None, None),
            P(("grp", "tm"), None, None),
            P(("grp", "tm"), None),
            P(),
            P(),
            P(),
            P(),
        ),
        out_specs=(P(("grp", "tm"), None, None), P("grp")),
        check_vma=False,
    )
```

profile of v0, /device:TPU:1, one launch (start us, length us, event | category | flops | bytes accessed | tf_op | source)
XLA Modules:
  0.0 47.2 jit_solution(3187077065276227671)
XLA Ops:
  0.6 1.4 %copy.9.pat_s.pat_v = s32[64,4]{1,0:T(8,128)} copy(s32[64,4]{0,1:T(4,128)} %param.13) | data formatting | bytes 2048 | tf_op args[6]
  2.0 39.4 %shard_map.86 = (f32[8,16,8192]{2,1,0:T(8,128)}, f32[8,128]{1,0:T(8,128)}) custom-call(s32[64,4]{1,0:T(8,128)} %copy.9.pat_s.pat_v, s32[64,4]{1,0:T(8,128)} %copy.9.pat_s.pat_v, f32[1,8192]{1,0:T(1,128)} %bitcast.4, f32[1,8192]{1,0:T(1,128)} %bitcast.5, f32[8,16,8192]{2,1,0:T(8,128)} %state.1, f32[8,16,8192]{2,1,0:T(8,128)} %forcing.1, f32[8,8192]{1,0:T(8,128)} %weight.1, ...), custom_call_target="tpu_custom_call" | custom-call | tf_op jit(solution)/shard_map/pallas_call | solution.py:249
  41.4 1.2 %slice_bitcast_fusion = f32[16]{0:T(128)} fusion(f32[8,128]{1,0:T(8,128)} %get-tuple-element.5), kind=kLoop, calls=%fused_computation | loop fusion | bytes 128 | tf_op jit(solution)/shard_map/squeeze | solution.py:284
  42.6 4.6 %copy.12 = f32[8,16,8192]{2,1,0:T(8,128)} copy(f32[8,16,8192]{2,1,0:T(8,128)} %get-tuple-element.8) | data formatting | bytes 8388608
where the time goes:
time: 47.5 us; the launch traced here: 47.2 us
  Pallas kernels  39.4 us (83%)
  local copies, waits for them, and re-layouts  7.17 us (15%)
  between operations  0.64 us (1%)
    pallas_call x1, Pallas kernels, shards(): pl.pallas_call(kernel, out_shape=(jax.ShapeDtypeStruct((days, samples, no...  39.4 us
    unnamed x2, local copies, waits for them, and re-layouts  5.99 us
    squeeze x1, local copies, waits for them, and re-layouts, shards(): return (gradient, density[0, :samples])  1.19 us

commit v1 on v0

--- a/solution.py
+++ b/solution.py
@@ -76,12 +76,14 @@
     none = blocks * links
     idx_v[...] = jnp.zeros_like(idx_v)
     finals = jnp.full((1, blocks), -1, jnp.int32)
-    columns = [pat_v[:, k : k + 1] for k in range(links)]
+    lines = [pat_v[k : k + 1, :] for k in range(links)]
+    columns = [
+        jnp.sum(jnp.where(lane == sub, line, 0), axis=1, keepdims=True) for line in lines
+    ]
     for k in range(links):
-        row = jnp.sum(jnp.where(lane == sub, columns[k], 0), axis=0, keepdims=True)
         found = jnp.full((1, blocks), -1, jnp.int32)
         for q in range(links):
-            hit = (columns[q] == row) & (sub < lane)
+            hit = (columns[q] == lines[k]) & (sub < lane)
             found = jnp.maximum(
                 found, jnp.max(jnp.where(hit, sub * links + q, -1), axis=0, keepdims=True)
             )
@@ -114,7 +116,7 @@
     loads[1].wait()
 
     def forward(i, total):
-        x = jnp.concatenate([xr[pat_s[i, k]] for k in range(links)], axis=1)
+        x = jnp.concatenate([xr[pat_s[k, i]] for k in range(links)], axis=1)
         acc = jnp.dot(x, b_v[i].reshape(links * width, width), preferred_element_type=F32)
         acc = acc.reshape(days, samples, width)
         c = cols(i)
@@ -249,8 +251,8 @@
     gradient, density = pl.pallas_call(
         kernel,
         out_shape=(
-            jax.ShapeDtypeStruct((days, samples, nodes), F32),
-            jax.ShapeDtypeStruct((8, width), F32),
+            pltpu.VMEM((days, samples, nodes), F32),
+            pltpu.VMEM((8, width), F32),
         ),
         in_specs=[pl.BlockSpec(memory_space=pltpu.SMEM), whole, whole, whole] + [away] * 4,
         out_specs=(whole, whole),
@@ -277,7 +279,7 @@
             collective_id=0, has_side_effects=True, vmem_limit_bytes=58 * 2**20
         ),
     )(
-        block_pattern, block_pattern,
+        block_pattern.T, block_pattern.T,
         prev_coupling.reshape(1, nodes), next_coupling.reshape(1, nodes),
         state, forcing, noise_weight, block_values,
     )

time: 47.5 us -> 40.3 us (0.85)
  local copies, waits for them, and re-layouts: 7.17 us -> 2.53 us
  Pallas kernels: 39.4 us -> 37 us
    unnamed x2 -> x1, local copies, waits for them, and re-layouts: 5.99 us -> 2.02 us
    pallas_call x1, Pallas kernels: 39.4 us -> 37 us  [shards(): pl.pallas_call(kernel, out_shape=(pltpu.VMEM((days, samples, nodes), F32)...]
    squeeze x1, local copies, waits for them, and re-layouts: 1.19 us -> 0.51 us  [shards(): return (gradient, density[0, :samples])]
where the time goes in v1:
time: 40.3 us; the launch traced here: 40.2 us
  Pallas kernels  37 us (92%)
  local copies, waits for them, and re-layouts  2.53 us (6%)
  between operations  0.64 us (2%)
    pallas_call x1, Pallas kernels, shards(): pl.pallas_call(kernel, out_shape=(pltpu.VMEM((days, samples, nodes), F32)...  37 us
    unnamed x1, local copies, waits for them, and re-layouts  2.02 us

profile of v1, /device:TPU:1, one launch (start us, length us, event | category | flops | bytes accessed | tf_op | source)
XLA Modules:
  0.0 40.2 jit_solution(2913092420441530879)
XLA Ops:
  0.6 37.0 %shard_map.86 = (f32[8,16,8192]{2,1,0:T(8,128)S(1)}, f32[8,128]{1,0:T(8,128)S(1)}) custom-call(s32[4,64]{1,0:T(4,128)} %bitcast.7, s32[4,64]{1,0:T(4,128)} %bitcast.8, f32[1,8192]{1,0:T(1,128)} %bitcast.5, f32[1,8192]{1,0:T(1,128)} %bitcast.6, f32[8,16,8192]{2,1,0:T(8,128)} %state.1, f32[8,16,8192]{2,1,0:T(8,128)} %forcing.1, f32[8,8192]{1,0:T(8,128)} %weight.1, ...), custom_call_target="tpu_custom_call" | custom-call | tf_op jit(solution)/shard_map/pallas_call | solution.py:251
  37.6 2.0 %copy.10 = f32[8,16,8192]{2,1,0:T(8,128)} copy(f32[8,16,8192]{2,1,0:T(8,128)S(1)} %get-tuple-element.6) | data formatting | bytes 8388608
  39.7 0.5 %slice_bitcast_fusion = f32[16]{0:T(128)} fusion(f32[8,128]{1,0:T(8,128)S(1)} %get-tuple-element.5), kind=kLoop, calls=%fused_computation | loop fusion | bytes 128 | tf_op jit(solution)/shard_map/squeeze | solution.py:286

commit v2 on v1

--- a/solution.py
+++ b/solution.py
@@ -17,7 +17,7 @@
     out, dens_out,
     s_v, f_v, w_v, b_v, xr, dr, dual, part, r_first, r_last, w_first, w_last,
     hs_prev, hs_next, hr_prev, hr_next, hw_prev, hw_next, dens, idx_v, idx_s,
-    load_sem, b_sem, idx_sem, halo_send, halo_recv, r_send, r_recv, d_send, d_recv,
+    load_sem, b_sem, idx_sem, halo_send, halo_recv, r_send, r_recv, d_send, d_recv, gate,
 ):
     days, samples, nodes = s_v.shape
     blocks, links, width, _ = b_v.shape
@@ -50,13 +50,22 @@
 
     barrier = pltpu.get_barrier_semaphore()
 
-    @pl.loop(1, n)
-    def _(s):
-        pl.semaphore_signal(
-            barrier, inc=1, device_id={"tm": lax.rem(me + s, n)}, device_id_type=MESH
-        )
-
-    pl.semaphore_wait(barrier, n - 1)
+    for peer in (left, right):
+        pl.semaphore_signal(barrier, inc=1, device_id={"tm": peer}, device_id_type=MESH)
+    pl.semaphore_wait(barrier, 2)
+
+    steps = gate.shape[0]
+
+    def announce(r):
+        for far in (1 << r, n - (1 << r)):
+            pl.semaphore_signal(
+                gate.at[r], inc=1, device_id={"tm": lax.rem(me + far, n)}, device_id_type=MESH
+            )
+
+    def learn(r):
+        pl.semaphore_wait(gate.at[r], 2)
+        if r < steps - 1:
+            announce(r + 1)
 
     def remote(src, dst, send, recv, target):
         return pltpu.make_async_remote_copy(
@@ -70,6 +79,7 @@
     ]
     for copy in halos:
         copy.start()
+    announce(0)
 
     lane = lax.broadcasted_iota(jnp.int32, (blocks, blocks), 1)
     sub = lax.broadcasted_iota(jnp.int32, (blocks, blocks), 0)
@@ -141,6 +151,8 @@
     total = jnp.zeros((samples, width), F32)
     for c in range(LOADS):
         b_load(c).wait()
+        if c < steps:
+            learn(c)
         total = lax.fori_loop(c * per_load, (c + 1) * per_load, forward, total, unroll=2)
         each = LOADS // PIECES
         if c % each == each - 1:
@@ -274,6 +286,7 @@
             sem((4,)), sem((4,)),
             sem((2, PIECES)), sem((2, PIECES)),
             sem((n,)), sem((n,)),
+            pltpu.SemaphoreType.REGULAR((max(1, (n // 2 - 1).bit_length()),)),
         ],
         compiler_params=pltpu.CompilerParams(
             collective_id=0, has_side_effects=True, vmem_limit_bytes=58 * 2**20

time: 40.3 us -> 37.5 us (0.931)
  Pallas kernels: 37 us -> 34.1 us
    pallas_call x1, Pallas kernels: 37 us -> 34.1 us  [shards(): pl.pallas_call(kernel, out_shape=(pltpu.VMEM((days, samples, nodes), F32)...]
where the time goes in v2:
time: 37.5 us; the launch traced here: 37.3 us
  Pallas kernels  34.1 us (91%)
  local copies, waits for them, and re-layouts  2.53 us (7%)
  between operations  0.64 us (2%)
    pallas_call x1, Pallas kernels, shards(): pl.pallas_call(kernel, out_shape=(pltpu.VMEM((days, samples, nodes), F32)...  34.1 us
    unnamed x1, local copies, waits for them, and re-layouts  2.02 us

profile of v2, /device:TPU:1, one launch (start us, length us, event | category | flops | bytes accessed | tf_op | source)
XLA Modules:
  0.0 37.3 jit_solution(5451205970704653420)
XLA Ops:
  0.6 34.1 %shard_map.86 = (f32[8,16,8192]{2,1,0:T(8,128)S(1)}, f32[8,128]{1,0:T(8,128)S(1)}) custom-call(s32[4,64]{1,0:T(4,128)} %bitcast.7, s32[4,64]{1,0:T(4,128)} %bitcast.8, f32[1,8192]{1,0:T(1,128)} %bitcast.5, f32[1,8192]{1,0:T(1,128)} %bitcast.6, f32[8,16,8192]{2,1,0:T(8,128)} %state.1, f32[8,16,8192]{2,1,0:T(8,128)} %forcing.1, f32[8,8192]{1,0:T(8,128)} %weight.1, ...), custom_call_target="tpu_custom_call" | custom-call | tf_op jit(solution)/shard_map/pallas_call | solution.py:263
  34.8 2.0 %copy.10 = f32[8,16,8192]{2,1,0:T(8,128)} copy(f32[8,16,8192]{2,1,0:T(8,128)S(1)} %get-tuple-element.6) | data formatting | bytes 8388608
  36.8 0.5 %slice_bitcast_fusion = f32[16]{0:T(128)} fusion(f32[8,128]{1,0:T(8,128)S(1)} %get-tuple-element.5), kind=kLoop, calls=%fused_computation | loop fusion | bytes 128 | tf_op jit(solution)/shard_map/squeeze | solution.py:299

commit v3 on v2

--- a/solution.py
+++ b/solution.py
@@ -153,7 +153,7 @@
         b_load(c).wait()
         if c < steps:
             learn(c)
-        total = lax.fori_loop(c * per_load, (c + 1) * per_load, forward, total, unroll=2)
+        total = lax.fori_loop(c * per_load, (c + 1) * per_load, forward, total, unroll=4)
         each = LOADS // PIECES
         if c % each == each - 1:
             for copy in r_copies(c // each):
@@ -203,7 +203,7 @@
             part[i * links + k] = part[idx_s[k, i]] + y[:, k * width : (k + 1) * width]
         return 0
 
-    lax.fori_loop(0, blocks, backward, 0, unroll=2)
+    lax.fori_loop(0, blocks, backward, 0, unroll=4)
 
     def gradient(j, _):
         adj = part[idx_s[links, j]].reshape(days, samples, width)
@@ -215,7 +215,7 @@
             out[d, :, c] = p * dual[d + 1, :, c] + q * dual[d - 1, :, c] - adj[d]
         return 0
 
-    lax.fori_loop(0, blocks, gradient, 0, unroll=2)
+    lax.fori_loop(0, blocks, gradient, 0, unroll=4)
 
     for copy in w_halos:
         copy.wait_recv()

time: 37.5 us -> 34.7 us (0.925)
  Pallas kernels: 34.1 us -> 31.4 us
    pallas_call x1, Pallas kernels: 34.1 us -> 31.4 us  [shards(): pl.pallas_call(kernel, out_shape=(pltpu.VMEM((days, samples, nodes), F32)...]
where the time goes in v3:
time: 34.7 us; the launch traced here: 34.6 us
  Pallas kernels  31.4 us (90%)
  local copies, waits for them, and re-layouts  2.53 us (7%)
  between operations  0.64 us (2%)
    pallas_call x1, Pallas kernels, shards(): pl.pallas_call(kernel, out_shape=(pltpu.VMEM((days, samples, nodes), F32)...  31.4 us
    unnamed x1, local copies, waits for them, and re-layouts  2.02 us

profile of v3, /device:TPU:1, one launch (start us, length us, event | category | flops | bytes accessed | tf_op | source)
XLA Modules:
  0.0 34.6 jit_solution(6429523598788023020)
XLA Ops:
  0.6 31.4 %shard_map.86 = (f32[8,16,8192]{2,1,0:T(8,128)S(1)}, f32[8,128]{1,0:T(8,128)S(1)}) custom-call(s32[4,64]{1,0:T(4,128)} %bitcast.7, s32[4,64]{1,0:T(4,128)} %bitcast.8, f32[1,8192]{1,0:T(1,128)} %bitcast.5, f32[1,8192]{1,0:T(1,128)} %bitcast.6, f32[8,16,8192]{2,1,0:T(8,128)} %state.1, f32[8,16,8192]{2,1,0:T(8,128)} %forcing.1, f32[8,8192]{1,0:T(8,128)} %weight.1, ...), custom_call_target="tpu_custom_call" | custom-call | tf_op jit(solution)/shard_map/pallas_call | solution.py:263
  32.0 2.0 %copy.10 = f32[8,16,8192]{2,1,0:T(8,128)} copy(f32[8,16,8192]{2,1,0:T(8,128)S(1)} %get-tuple-element.6) | data formatting | bytes 8388608
  34.1 0.5 %slice_bitcast_fusion = f32[16]{0:T(128)} fusion(f32[8,128]{1,0:T(8,128)S(1)} %get-tuple-element.5), kind=kLoop, calls=%fused_computation | loop fusion | bytes 128 | tf_op jit(solution)/shard_map/squeeze | solution.py:299
